TPU v7x, 32 devices: a whole 2x2x4 slice. The times are simulated.
32 devices in a mesh: slab: 8 (over z, x), orb: 4 (over y, core).
Axes of the slice: x: 2, y: 2, z: 4, core: 2. Of those that a mesh axis runs over, the one named last changes fastest.
Arguments:
- orbitals: bfloat16 [8, 4, 1, 64, 2304], P(None, 'orb', None, 'slab'), may hold values from -6 to 6
- potential: float32 [64, 2304], P('slab'), may hold values from -1.5 to 0.5
- partners: int32 [8, 4, 1, 2], P('slab', 'orb'), may hold values from 0 to 31, as said below
- pair_valid: int32 [8, 4, 1, 2], P('slab', 'orb'), may hold values from 0 to 1, as said below
Outputs:
- action: bfloat16 [8, 4, 1, 64, 2304], P(None, 'orb', None, 'slab')
Inputs may be any that keep to these rules, and one draw needn't show every extreme that they name: partners names, for orbital number n = (a * 4 + b) + r, an orbital number that differs from n by 1 to 1 along the cyclic order of the 32 orbitals: ahead of n in even slots, behind n in odd slots; a partner may be listed more than once. `pair_valid`: slot 0 of every orbital is used.
All inputs are finite; a program needn't handle non-finite values.
Results may differ from a plain program's by a relative error of at most 0.001.
Values may be sent and summed in bfloat16 or wider, within the bound.
A program may use at most 64 MiB of HBM per device.

v0:
```python
import math

import jax
import jax.numpy as jnp
from jax import lax
from jax.sharding import PartitionSpec as P

NX = 48
NY = 48
NZ = 64


stencil_weights = (-205.0 / 72.0, 8.0 / 5.0, -1.0 / 5.0, 8.0 / 315.0, -1.0 / 560.0)
screening = 0.11
mixing = 0.25


def with_halo(block, sides, width):
    for axis, dim in sides:
        count = lax.axis_size(axis)
        forward = [(i, i + 1) for i in range(count - 1)]
        forward.append((count - 1, 0))
        backward = [(target, source) for source, target in forward]
        low = lax.ppermute(
            lax.slice_in_dim(block, block.shape[dim] - width, None, axis=dim), axis, forward
        )
        high = lax.ppermute(lax.slice_in_dim(block, 0, width, axis=dim), axis, backward)
        block = jnp.concatenate([low, block, high], axis=dim)
    return block


def squared_wave(length):
    grid = jnp.arange(length, dtype=jnp.int32)
    folded = jnp.minimum(grid, length - grid).astype(jnp.float32)
    return 2.0 * math.pi * folded / length * (2.0 * math.pi * folded / length)


def screened_kernel(depth, rows, cols):
    wave = (
        squared_wave(depth)[:, None, None]
        + squared_wave(rows)[None, :, None]
        + squared_wave(cols)[None, None, :]
    )
    safe = jnp.where(wave > 0, wave, 1.0)
    inner = 4.0 * math.pi / safe * (1.0 - jnp.exp(-safe / (4.0 * screening * screening)))
    return jnp.where(wave > 0, inner, math.pi / (screening * screening))


def hartley(length):
    grid = jnp.arange(length, dtype=jnp.int32)
    phase = grid[:, None] * grid[None, :] % length
    angle = phase.astype(jnp.float32) * (2.0 * math.pi / length)
    return jnp.cos(angle) + jnp.sin(angle)


def rotate_apply(data, matrix, middle):
    product = jnp.dot(
        matrix, data, precision=lax.Precision.HIGHEST, preferred_element_type=jnp.float32
    )
    leading = product.shape[0]
    cubed = product.reshape(leading, middle, product.shape[1] // middle)
    turned = jnp.transpose(cubed, (1, 2, 0))
    return turned.reshape(middle, -1)


def hartley_three(data, tables):
    depth_table, row_table, col_table = tables
    step_one = rotate_apply(data, depth_table, row_table.shape[0])
    step_two = rotate_apply(step_one, row_table, col_table.shape[0])
    return rotate_apply(step_two, col_table, depth_table.shape[0])


def pair_potential(density, tables, kernel):
    return hartley_three(kernel * hartley_three(density, tables), tables)


def lateral_second(field, width_x):
    column = jnp.arange(field.shape[-1], dtype=jnp.int32) % width_x
    total = 2.0 * stencil_weights[0] * field
    for reach in range(1, 5):
        along_y = jnp.roll(field, reach * width_x, -1) + jnp.roll(field, -reach * width_x, -1)
        upper = jnp.where(
            column + reach < width_x,
            jnp.roll(field, -reach, -1),
            jnp.roll(field, width_x - reach, -1),
        )
        lower = jnp.where(
            column >= reach, jnp.roll(field, reach, -1), jnp.roll(field, reach - width_x, -1)
        )
        total = total + stencil_weights[reach] * (along_y + upper + lower)
    return total


def vertical_part(column, depth):
    total = stencil_weights[0] * column[:, :, :, 4 : 4 + depth]
    for reach in range(1, 5):
        above = column[:, :, :, 4 + reach : 4 + reach + depth]
        below = column[:, :, :, 4 - reach : 4 - reach + depth]
        total = total + stencil_weights[reach] * (above + below)
    return total


def planes_of(data):
    return with_halo(data, (("slab", 3),), 2)


def local(orbitals, potential, partners, pair_valid):
    width = orbitals.shape[2]
    depth = orbitals.shape[3]
    count = partners.shape[3]
    values = orbitals.astype(jnp.float32)
    laplace = lateral_second(values, NX)
    near = planes_of(orbitals)
    rims = jnp.concatenate([near[:, :, :, 4:6], near[:, :, :, depth - 2 : depth]], axis=3)
    far = planes_of(rims)
    column = jnp.concatenate([far[:, :, :, 0:2], near, far[:, :, :, 6:8]], axis=3).astype(
        jnp.float32
    )
    laplace = laplace + vertical_part(column, depth)
    owned = lax.all_to_all(orbitals, "slab", split_axis=0, concat_axis=3, tiled=True)
    owned = owned.reshape(width, NZ, NY * NX)
    extended = with_halo(owned, ((("slab", "orb"), 0),), width)
    chain = lax.axis_index("slab") * lax.axis_size("orb") + lax.axis_index("orb")
    total_orbitals = width * lax.axis_size("slab") * lax.axis_size("orb")
    tables = (hartley(NZ), hartley(NY), hartley(NX))
    kernel = screened_kernel(NZ, NY, NX).reshape(NZ, NY * NX) / float(NZ * NY * NX)
    own_lists = partners.reshape(width, count)
    own_flags = pair_valid.reshape(width, count)
    offsets = (own_lists - (chain - 1) * width) % total_orbitals
    weights = own_flags.astype(jnp.float32)

    def pair_turn(slot, accum):
        lister = slot // count
        column_index = slot % count
        partner_row = offsets[lister, column_index]
        weight = weights[lister, column_index]
        first = lax.dynamic_index_in_dim(extended, width + lister, 0, keepdims=False).astype(
            jnp.float32
        )
        second = lax.dynamic_index_in_dim(extended, partner_row, 0, keepdims=False).astype(
            jnp.float32
        )
        field = pair_potential(first * second, tables, kernel) * weight
        accum = accum.at[width + lister].add(field * second)
        accum = accum.at[partner_row].add(field * first)
        return accum

    start = jnp.zeros((3 * width, NZ, NY * NX), jnp.float32)
    partial_value = lax.fori_loop(0, width * count, pair_turn, start)
    outward = jnp.concatenate(
        [partial_value[0:width], partial_value[2 * width : 3 * width]], axis=0
    )
    inward = with_halo(outward, ((("slab", "orb"), 0),), width)
    exchange_term = (
        partial_value[width : 2 * width] + inward[0:width] + inward[3 * width : 4 * width]
    )
    outgoing = -mixing * exchange_term
    outgoing = outgoing.reshape(1, 1, width, NZ, NY * NX)
    returned = lax.all_to_all(outgoing, "slab", split_axis=3, concat_axis=0, tiled=True)
    result = -0.5 * laplace + potential[None, None, None, :, :] * values + returned
    return result.astype(jnp.bfloat16)


def solution(mesh):
    in_specs = (
        P(None, "orb", None, "slab", None),
        P("slab", None),
        P("slab", "orb", None, None),
        P("slab", "orb", None, None),
    )
    out_specs = P(None, "orb", None, "slab", None)
    return jax.shard_map(local, mesh=mesh, in_specs=in_specs, out_specs=out_specs, check_vma=False)
```

profile of v0, /device:TPU:5, one launch (start us, length us, event | category | flops | bytes accessed | tf_op | source)
XLA Modules:
  0.0 154.8 jit_solution(17420521212317398469)
XLA Ops:
  0.0 5.7 %all-to-all-start = ((bf16[8,1,1,8,2304]{4,3,2,1,0:T(8,128)(2,1)}), bf16[8,1,1,8,2304]{4,3,2,1,0:T(8,128)(2,1)S(1)}, u32[]{:S(2)}, u32[]{:S(2)}) async-start(bf16[8,1,1,8,2304]{4,3,2,1,0:T(8,128)(2,1)} %param.10), calls=%async_computation | async-start | bytes 589824 | tf_op jit(solution)/shard_map/all_to_all | solution.py:120
  5.7 2.2 %fusion.136 = (bf16[8,1,1,2,2304]{4,3,2,1,0:T(2,128)(2,1)}, bf16[8,1,1,2,2304]{4,3,2,1,0:T(2,128)(2,1)}, bf16[8,1,1,2,2304]{4,3,2,1,0:T(2,128)(2,1)}, bf16[8,1,1,2,2304]{4,3,2,1,0:T(2,128)(2,1)}) fusion(bf16[8,1,1,8,2304]{4,3,2,1,0:T(8,128)(2,1)} %param.10), kind=kLoop, calls=%fused_computation.192 | loop fusion | bytes 589824 | tf_op jit(solution)/shard_map/slice | solution.py:114
  7.9 1.5 collective-permute-start
  9.4 1.2 collective-permute-start.1
  10.6 3.0 %collective-permute-start.2 = (bf16[8,1,1,2,2304]{4,3,2,1,0:T(2,128)(2,1)}, bf16[8,1,1,2,2304]{4,3,2,1,0:T(2,128)(2,1)}, u32[]{:S(2)}, u32[]{:S(2)}) collective-permute-start(bf16[8,1,1,2,2304]{4,3,2,1,0:T(2,128)(2,1)} %get-tuple-element.398), channel_id=1, source_target_pairs={{4,0},{8,4},{12,8},{16,12},{20,16},{24,20},{28,24},{0,28},{5,1},{9... | collective-permute-start | bytes 221192 | tf_op jit(solution)/shard_map/ppermute | solution.py:27
  13.6 1.2 fusion.112
  14.7 1.2 fusion.115
  15.9 1.2 fusion.118
  17.1 1.1 fusion.121
  18.2 1.2 fusion.124
  19.4 1.1 fusion.127
  20.5 1.2 fusion.128
  21.7 1.2 fusion.130
  22.9 1.1 fusion.133
  32.9 1.1 fusion.134
  34.4 1.7 %collective-permute-start.5 = (bf16[1,64,2304]{2,1,0:T(8,128)(2,1)S(1)}, bf16[1,64,2304]{2,1,0:T(8,128)(2,1)S(1)}, u32[]{:S(2)}, u32[]{:S(2)}) collective-permute-start(bf16[1,64,2304]{2,1,0:T(8,128)(2,1)S(1)} %bitcast.91), channel_id=1, source_target_pairs={{1,0},{2,1},{3,2},{4,3},{5,4},{6,5},{7,6},{8,7},{9,8},{10,9},{11,1... | collective-permute-start | bytes 884744 | tf_op jit(solution)/shard_map/ppermute | solution.py:27
  38.2 3.4 %collective-permute-done.5 = bf16[1,64,2304]{2,1,0:T(8,128)(2,1)S(1)} collective-permute-done((bf16[1,64,2304]{2,1,0:T(8,128)(2,1)S(1)}, bf16[1,64,2304]{2,1,0:T(8,128)(2,1)S(1)}, u32[]{:S(2)}, u32[]{:S(2)}) %collective-permute-start.5) | collective-permute-done | bytes 294944 | tf_op jit(solution)/shard_map/ppermute | solution.py:27
  41.6 1.0 pad_maximum_fusion
  42.6 1.4 broadcast_in_dim.57
  44.0 58.9 %while.19 = (s32[]{:T(128)}, f32[3,64,2304]{2,1,0:T(8,128)}, bf16[3,64,2304]{2,1,0:T(8,128)(2,1)}, s32[1,2]{1,0:T(1,128)S(1)}, f32[1,2]{1,0:T(1,128)}, /*index=5...) while((s32[]{:T(128)}, f32[3,64,2304]{2,1,0:T(8,128)}, ...), condition=%wide.region_3.4_spmd.clone.clone, body=%wide.region_0.3_spmd.clone.clone.sunk | while | flops 569837632 | bytes 34825848 | solution.py:149
  46.3 1.9 %convolution_bitcast_fusion.10 = f32[64,2304]{1,0:T(8,128)S(1)} fusion(bf16[3,64,2304]{2,1,0:T(8,128)(2,1)} %get-tuple-element.488, s32[]{:T(128)} %select_n.376, s32[]{:T(128)} %select_n.373), kind=kOutput, calls=%fused_computation.4.clone.1 | convolution fusion | flops 113750016 | bytes 1180672 | tf_op jit(solution)/shard_map/while/body/eval_jaxpr/dot_general | solution.py:57
  48.2 1.0 reshape.1132
  51.4 1.1 reshape.1134
  54.8 1.5 reshape.1136
  57.5 1.1 convolution_bitcast_fusion.13
  61.8 1.1 reshape.1139
  63.6 1.4 fusion.156
  68.0 2.7 %fusion.157 = f32[3,64,2304]{2,1,0:T(8,128)} fusion(f32[3,64,2304]{2,1,0:T(8,128)} %get-tuple-element.472, s32[]{:T(128)} %select_n.373, f32[1,64,2304]{2,1,0:T(8,128)S(1)} %mul.832, pred[]{:T(512)} %get-tuple-element.454, bf16[3,64,2304]{2,1,0:T(8,128)(2,1)} %get-tuple-element.488, s32[]{:T(128)} %select_n.376), kind=kLoop, calls=%fused_computation.20.clone.1 | loop fusion | flops 589824 | bytes 2065920 | tf_op jit(solution)/shard_map/while/body/eval_jaxpr/scatter-add | solution.py:144
  70.7 2.7 %fusion.158 = f32[3,64,2304]{2,1,0:T(8,128)} fusion(f32[3,64,2304]{2,1,0:T(8,128)} %fusion.157, s32[]{:T(128)} %select_n.376, f32[1,64,2304]{2,1,0:T(8,128)S(1)} %mul.832, pred[]{:T(512)} %get-tuple-element.455, bf16[3,64,2304]{2,1,0:T(8,128)(2,1)} %get-tuple-element.488, s32[]{:T(128)} %select_n.373), kind=kLoop, calls=%fused_computation.21.clone.1 | loop fusion | flops 589824 | bytes 2065920 | tf_op jit(solution)/shard_map/while/body/eval_jaxpr/scatter-add | solution.py:145
  75.7 1.9 %convolution_bitcast_fusion.10 = f32[64,2304]{1,0:T(8,128)S(1)} fusion(bf16[3,64,2304]{2,1,0:T(8,128)(2,1)} %get-tuple-element.488, s32[]{:T(128)} %select_n.376, s32[]{:T(128)} %select_n.373), kind=kOutput, calls=%fused_computation.4.clone.1 | convolution fusion | flops 113750016 | bytes 1180672 | tf_op jit(solution)/shard_map/while/body/eval_jaxpr/dot_general | solution.py:57
  80.8 1.1 reshape.1134
  84.3 1.5 reshape.1136
  86.9 1.1 convolution_bitcast_fusion.13
  91.2 1.1 reshape.1139
  93.0 1.4 fusion.156
  97.5 2.7 %fusion.157 = f32[3,64,2304]{2,1,0:T(8,128)} fusion(f32[3,64,2304]{2,1,0:T(8,128)} %get-tuple-element.472, s32[]{:T(128)} %select_n.373, f32[1,64,2304]{2,1,0:T(8,128)S(1)} %mul.832, pred[]{:T(512)} %get-tuple-element.454, bf16[3,64,2304]{2,1,0:T(8,128)(2,1)} %get-tuple-element.488, s32[]{:T(128)} %select_n.376), kind=kLoop, calls=%fused_computation.20.clone.1 | loop fusion | flops 589824 | bytes 2065920 | tf_op jit(solution)/shard_map/while/body/eval_jaxpr/scatter-add | solution.py:144
  100.1 2.8 %fusion.158 = f32[3,64,2304]{2,1,0:T(8,128)} fusion(f32[3,64,2304]{2,1,0:T(8,128)} %fusion.157, s32[]{:T(128)} %select_n.376, f32[1,64,2304]{2,1,0:T(8,128)S(1)} %mul.832, pred[]{:T(512)} %get-tuple-element.455, bf16[3,64,2304]{2,1,0:T(8,128)(2,1)} %get-tuple-element.488, s32[]{:T(128)} %select_n.373), kind=kLoop, calls=%fused_computation.21.clone.1 | loop fusion | flops 589824 | bytes 2065920 | tf_op jit(solution)/shard_map/while/body/eval_jaxpr/scatter-add | solution.py:145
  102.9 2.7 %copy.18 = f32[3,64,2304]{2,0,1:T(4,128)S(1)} copy(f32[3,64,2304]{2,1,0:T(8,128)} %get-tuple-element.285) | data formatting | bytes 3538944 | tf_op jit(solution)/shard_map/while | solution.py:149
  106.6 3.8 %collective-permute-start.7 = (f32[1,64,2304]{2,0,1:T(1,128)S(1)}, f32[1,64,2304]{2,0,1:T(1,128)S(1)}, u32[]{:S(2)}, u32[]{:S(2)}) collective-permute-start(f32[1,64,2304]{2,0,1:T(1,128)S(1)} %get-tuple-element.348), channel_id=1, source_target_pairs={{1,0},{2,1},{3,2},{4,3},{5,4},{6,5},{7,6},{8,7},{9,8},{10,9},{11,1... | collective-permute-start | bytes 1769480 | tf_op jit(solution)/shard_map/ppermute | solution.py:27
  110.4 1.1 fusion.116
  111.5 1.9 %collective-permute-done.6 = f32[1,64,2304]{2,0,1:T(1,128)S(1)} collective-permute-done((f32[1,64,2304]{2,0,1:T(1,128)S(1)}, f32[1,64,2304]{2,0,1:T(1,128)S(1)}, u32[]{:S(2)}, u32[]{:S(2)}) %collective-permute-start.6) | collective-permute-done | bytes 589856 | tf_op jit(solution)/shard_map/ppermute | solution.py:24
  113.4 8.3 %collective-permute-start.3 = (bf16[8,1,1,2,2304]{4,3,2,1,0:T(2,128)(2,1)S(1)}, bf16[8,1,1,2,2304]{4,3,2,1,0:T(2,128)(2,1)S(1)}, u32[]{:S(2)}, u32[]{:S(2)}) collective-permute-start(bf16[8,1,1,2,2304]{4,3,2,1,0:T(2,128)(2,1)S(1)} %copy-done.7), channel_id=1, source_target_pairs={{4,0},{8,4},{12,8},{16,12},{20,16},{24,20},{28,24},{0,28},{5,1},{9... | collective-permute-start | bytes 221192 | tf_op jit(solution)/shard_map/ppermute | solution.py:27
  121.8 2.1 %multiply_bitcast_fusion = f32[1,1,1,64,2304]{4,2,1,0,3:T(1,128)} fusion(f32[1,64,2304]{2,0,1:T(1,128)S(1)} %collective-permute-done.7, f32[1,64,2304]{2,0,1:T(1,128)S(1)} %collective-permute-done.6, f32[3,64,2304]{2,0,1:T(4,128)S(1)} %copy.18), kind=kLoop, calls=%fused_computation.139 | loop fusion | flops 442368 | bytes 2359296 | tf_op jit(solution)/shard_map/reshape | solution.py:158
  123.8 7.4 %all-to-all-start.1 = ((f32[1,1,1,64,2304]{4,2,1,0,3:T(1,128)}), f32[1,1,1,64,2304]{4,2,1,0,3:T(1,128)S(1)}, u32[]{:S(2)}, u32[]{:S(2)}) async-start(f32[1,1,1,64,2304]{4,2,1,0,3:T(1,128)} %multiply_bitcast_fusion), calls=%async_computation.1 | async-start | bytes 1179648 | tf_op jit(solution)/shard_map/all_to_all | solution.py:159
  131.9 1.1 fusion.122
  133.8 5.2 %concatenate.346 = bf16[8,1,1,16,2304]{4,3,2,1,0:T(8,128)(2,1)S(1)} concatenate(bf16[8,1,1,2,2304]{4,3,2,1,0:T(2,128)(2,1)} %collective-permute-done, bf16[8,1,1,2,2304]{4,3,2,1,0:T(2,128)(2,1)} %collective-permute-done.1, bf16[8,1,1,8,2304]{4,3,2,1,0:T(8,128)(2,1)S(1)} %copy-done, bf16[8,1,1,2,2304]{4,3,2,1,0:T(2,128)(2,1)} %collective-permute-done.2, ...), dimensions={3} | concatenate | bytes 1179648 | tf_op jit(solution)/shard_map/concatenate | solution.py:116
  139.0 8.0 %all-to-all-done.1 = f32[1,1,1,64,2304]{4,2,1,0,3:T(1,128)S(1)} async-done(((f32[1,1,1,64,2304]{4,2,1,0,3:T(1,128)}), f32[1,1,1,64,2304]{4,2,1,0,3:T(1,128)S(1)}, u32[]{:S(2)}, u32[]{:S(2)}) %all-to-all-start.1) | async-done | bytes 589856 | tf_op jit(solution)/shard_map/all_to_all | solution.py:159
  147.1 7.5 %fusion.74 = bf16[8,1,1,8,2304]{4,3,2,1,0:T(8,128)(2,1)} fusion(f32[8,1,1,16,2304]{4,3,2,1,0:T(8,128)S(1)} %convert_element_type.92, f32[8,1,1,8,2256]{4,3,2,1,0:T(8,128)} %get-tuple-element.394, f32[8,1,1,8,48]{4,3,2,1,0:T(8,128)} %get-tuple-element.396, f32[8,1,1,8,48]{4,3,2,1,0:T(8,128)} %get-tuple-element.395, ...), kind=kLoop, calls=%fused_computation.100 | loop fusion | flops 10764288 | bytes 20736000 | tf_op jit(solution)/shard_map/convert_element_type | solution.py:161
  (119 shorter events, 40.7 us)
Async XLA Ops:
  0.0 13.5 %copy-start = (bf16[8,1,1,8,2304]{4,3,2,1,0:T(8,128)(2,1)S(1)}, bf16[8,1,1,8,2304]{4,3,2,1,0:T(8,128)(2,1)}, u32[]{:S(2)}) copy-start(bf16[8,1,1,8,2304]{4,3,2,1,0:T(8,128)(2,1)} %param.10) | copy-start | bytes 884740
  0.0 34.0 %all-to-all-start = ((bf16[8,1,1,8,2304]{4,3,2,1,0:T(8,128)(2,1)}), bf16[8,1,1,8,2304]{4,3,2,1,0:T(8,128)(2,1)S(1)}, u32[]{:S(2)}, u32[]{:S(2)}) async-start(bf16[8,1,1,8,2304]{4,3,2,1,0:T(8,128)(2,1)} %param.10), calls=%async_computation | async-start | bytes 589824 | tf_op jit(solution)/shard_map/all_to_all | solution.py:120
  7.9 125.8 %collective-permute-start = (bf16[8,1,1,2,2304]{4,3,2,1,0:T(2,128)(2,1)}, bf16[8,1,1,2,2304]{4,3,2,1,0:T(2,128)(2,1)}, u32[]{:S(2)}, u32[]{:S(2)}) collective-permute-start(bf16[8,1,1,2,2304]{4,3,2,1,0:T(2,128)(2,1)} %get-tuple-element.400), channel_id=1, source_target_pairs={{0,4},{4,8},{8,12},{12,16},{16,20},{20,24},{24,28},{28,0},{1,5},{5... | collective-permute-start | bytes 221192 | tf_op jit(solution)/shard_map/ppermute | solution.py:24
  9.4 124.4 %collective-permute-start.1 = (bf16[8,1,1,2,2304]{4,3,2,1,0:T(2,128)(2,1)}, bf16[8,1,1,2,2304]{4,3,2,1,0:T(2,128)(2,1)}, u32[]{:S(2)}, u32[]{:S(2)}) collective-permute-start(bf16[8,1,1,2,2304]{4,3,2,1,0:T(2,128)(2,1)} %get-tuple-element.399), channel_id=1, source_target_pairs={{0,4},{4,8},{8,12},{12,16},{16,20},{20,24},{24,28},{28,0},{1,5},{5... | collective-permute-start | bytes 221192 | tf_op jit(solution)/shard_map/ppermute | solution.py:24
  10.6 123.2 %collective-permute-start.2 = (bf16[8,1,1,2,2304]{4,3,2,1,0:T(2,128)(2,1)}, bf16[8,1,1,2,2304]{4,3,2,1,0:T(2,128)(2,1)}, u32[]{:S(2)}, u32[]{:S(2)}) collective-permute-start(bf16[8,1,1,2,2304]{4,3,2,1,0:T(2,128)(2,1)} %get-tuple-element.398), channel_id=1, source_target_pairs={{4,0},{8,4},{12,8},{16,12},{20,16},{24,20},{28,24},{0,28},{5,1},{9... | collective-permute-start | bytes 221192 | tf_op jit(solution)/shard_map/ppermute | solution.py:27
  22.9 9.4 %copy-start.13 = (s32[1,1,1,2]{3,2,1,0:T(1,128)S(1)}, s32[1,1,1,2]{3,2,1,0:T(1,128)}, u32[]{:S(2)}) copy-start(s32[1,1,1,2]{3,2,1,0:T(1,128)} %param.13) | copy-start | bytes 28
  22.9 10.0 %copy-start.14 = (s32[1,1,1,2]{3,2,1,0:T(1,128)S(1)}, s32[1,1,1,2]{3,2,1,0:T(1,128)}, u32[]{:S(2)}) copy-start(s32[1,1,1,2]{3,2,1,0:T(1,128)} %param.12) | copy-start | bytes 28
  34.0 4.1 %collective-permute-start.4 = (bf16[1,64,2304]{2,1,0:T(8,128)(2,1)S(1)}, bf16[1,64,2304]{2,1,0:T(8,128)(2,1)S(1)}, u32[]{:S(2)}, u32[]{:S(2)}) collective-permute-start(bf16[1,64,2304]{2,1,0:T(8,128)(2,1)S(1)} %bitcast.90), channel_id=1, source_target_pairs={{0,1},{1,2},{2,3},{3,4},{4,5},{5,6},{6,7},{7,8},{8,9},{9,10},{10,1... | collective-permute-start | bytes 884744 | tf_op jit(solution)/shard_map/ppermute | solution.py:24
  34.4 7.2 %collective-permute-start.5 = (bf16[1,64,2304]{2,1,0:T(8,128)(2,1)S(1)}, bf16[1,64,2304]{2,1,0:T(8,128)(2,1)S(1)}, u32[]{:S(2)}, u32[]{:S(2)}) collective-permute-start(bf16[1,64,2304]{2,1,0:T(8,128)(2,1)S(1)} %bitcast.91), channel_id=1, source_target_pairs={{1,0},{2,1},{3,2},{4,3},{5,4},{6,5},{7,6},{8,7},{9,8},{10,9},{11,1... | collective-permute-start | bytes 884744 | tf_op jit(solution)/shard_map/ppermute | solution.py:27
  37.5 6.5 %copy-start.8 = (s32[3]{0:T(128)S(1)}, s32[3]{0:T(128)}, u32[]{:S(2)}) copy-start(s32[3]{0:T(128)} %constant.257.clone.3) | copy-start | bytes 40
  44.0 2.3 %copy-start.16 = (s32[1,2]{1,0:T(1,128)}, s32[1,2]{1,0:T(1,128)S(1)}, u32[]{:S(2)}) copy-start(s32[1,2]{1,0:T(1,128)S(1)} %get-tuple-element.489) | copy-start | bytes 28 | tf_op jit(solution)/shard_map/while
  56.3 1.2 copy-start.1
  61.3 1.6 %copy-start.15 = (f32[1,2]{1,0:T(1,128)S(1)}, f32[1,2]{1,0:T(1,128)}, u32[]{:S(2)}) copy-start(f32[1,2]{1,0:T(1,128)} %get-tuple-element.490) | copy-start | bytes 28 | tf_op jit(solution)/shard_map/while
  68.0 5.4 %copy-start.17 = (s32[1,2]{1,0:T(1,128)S(1)}, s32[1,2]{1,0:T(1,128)}, u32[]{:S(2)}) copy-start(s32[1,2]{1,0:T(1,128)} %copy-done.16) | copy-start | bytes 28 | tf_op jit(solution)/shard_map/while
  73.4 2.3 %copy-start.16 = (s32[1,2]{1,0:T(1,128)}, s32[1,2]{1,0:T(1,128)S(1)}, u32[]{:S(2)}) copy-start(s32[1,2]{1,0:T(1,128)S(1)} %get-tuple-element.489) | copy-start | bytes 28 | tf_op jit(solution)/shard_map/while
  85.7 1.2 copy-start.1
  90.7 1.6 %copy-start.15 = (f32[1,2]{1,0:T(1,128)S(1)}, f32[1,2]{1,0:T(1,128)}, u32[]{:S(2)}) copy-start(f32[1,2]{1,0:T(1,128)} %get-tuple-element.490) | copy-start | bytes 28 | tf_op jit(solution)/shard_map/while
  97.5 5.4 %copy-start.17 = (s32[1,2]{1,0:T(1,128)S(1)}, s32[1,2]{1,0:T(1,128)}, u32[]{:S(2)}) copy-start(s32[1,2]{1,0:T(1,128)} %copy-done.16) | copy-start | bytes 28 | tf_op jit(solution)/shard_map/while
  105.6 7.9 %copy-start.7 = (bf16[8,1,1,2,2304]{4,3,2,1,0:T(2,128)(2,1)S(1)}, bf16[8,1,1,2,2304]{4,3,2,1,0:T(2,128)(2,1)}, u32[]{:S(2)}) copy-start(bf16[8,1,1,2,2304]{4,3,2,1,0:T(2,128)(2,1)} %get-tuple-element.397) | copy-start | bytes 221188
  106.5 6.9 %collective-permute-start.6 = (f32[1,64,2304]{2,0,1:T(1,128)S(1)}, f32[1,64,2304]{2,0,1:T(1,128)S(1)}, u32[]{:S(2)}, u32[]{:S(2)}) collective-permute-start(f32[1,64,2304]{2,0,1:T(1,128)S(1)} %get-tuple-element.347), channel_id=1, source_target_pairs={{0,1},{1,2},{2,3},{3,4},{4,5},{5,6},{6,7},{7,8},{8,9},{9,10},{10,1... | collective-permute-start | bytes 1769480 | tf_op jit(solution)/shard_map/ppermute | solution.py:24
  106.6 15.2 %collective-permute-start.7 = (f32[1,64,2304]{2,0,1:T(1,128)S(1)}, f32[1,64,2304]{2,0,1:T(1,128)S(1)}, u32[]{:S(2)}, u32[]{:S(2)}) collective-permute-start(f32[1,64,2304]{2,0,1:T(1,128)S(1)} %get-tuple-element.348), channel_id=1, source_target_pairs={{1,0},{2,1},{3,2},{4,3},{5,4},{6,5},{7,6},{8,7},{9,8},{10,9},{11,1... | collective-permute-start | bytes 1769480 | tf_op jit(solution)/shard_map/ppermute | solution.py:27
  113.4 20.3 %collective-permute-start.3 = (bf16[8,1,1,2,2304]{4,3,2,1,0:T(2,128)(2,1)S(1)}, bf16[8,1,1,2,2304]{4,3,2,1,0:T(2,128)(2,1)S(1)}, u32[]{:S(2)}, u32[]{:S(2)}) collective-permute-start(bf16[8,1,1,2,2304]{4,3,2,1,0:T(2,128)(2,1)S(1)} %copy-done.7), channel_id=1, source_target_pairs={{4,0},{8,4},{12,8},{16,12},{20,16},{24,20},{28,24},{0,28},{5,1},{9... | collective-permute-start | bytes 221192 | tf_op jit(solution)/shard_map/ppermute | solution.py:27
  123.8 23.2 %all-to-all-start.1 = ((f32[1,1,1,64,2304]{4,2,1,0,3:T(1,128)}), f32[1,1,1,64,2304]{4,2,1,0,3:T(1,128)S(1)}, u32[]{:S(2)}, u32[]{:S(2)}) async-start(f32[1,1,1,64,2304]{4,2,1,0,3:T(1,128)} %multiply_bitcast_fusion), calls=%async_computation.1 | async-start | bytes 1179648 | tf_op jit(solution)/shard_map/all_to_all | solution.py:159
  133.1 14.0 %copy-start.2 = (f32[8,1,1,8,2260]{4,3,2,1,0:T(8,128)S(1)}, f32[8,1,1,8,2260]{4,3,2,1,0:T(8,128)}, u32[]{:S(2)}) copy-start(f32[8,1,1,8,2260]{4,3,2,1,0:T(8,128)} %get-tuple-element.349) | copy-start | bytes 1735684
  133.1 14.0 %copy-start.3 = (f32[8,1,1,8,192]{4,3,2,1,0:T(8,128)S(1)}, f32[8,1,1,8,192]{4,3,2,1,0:T(8,128)}, u32[]{:S(2)}) copy-start(f32[8,1,1,8,192]{4,3,2,1,0:T(8,128)} %get-tuple-element.360) | copy-start | bytes 147460
  133.1 14.0 %copy-start.4 = (f32[8,1,1,8,144]{4,3,2,1,0:T(8,128)S(1)}, f32[8,1,1,8,144]{4,3,2,1,0:T(8,128)}, u32[]{:S(2)}) copy-start(f32[8,1,1,8,144]{4,3,2,1,0:T(8,128)} %get-tuple-element.371) | copy-start | bytes 110596
  133.1 14.0 %copy-start.5 = (f32[8,1,1,8,144]{4,3,2,1,0:T(8,128)S(1)}, f32[8,1,1,8,144]{4,3,2,1,0:T(8,128)}, u32[]{:S(2)}) copy-start(f32[8,1,1,8,144]{4,3,2,1,0:T(8,128)} %get-tuple-element.372) | copy-start | bytes 110596
  133.1 14.0 %copy-start.6 = (f32[8,1,1,8,44]{4,3,2,1,0:T(8,128)S(1)}, f32[8,1,1,8,44]{4,3,2,1,0:T(8,128)}, u32[]{:S(2)}) copy-start(f32[8,1,1,8,44]{4,3,2,1,0:T(8,128)} %get-tuple-element.351) | copy-start | bytes 33796
  133.1 14.0 %copy-start.9 = (pred[2304]{0:T(1024)(128)(4,1)S(1)}, pred[2304]{0:T(1024)(128)(4,1)}, u32[]{:S(2)}) copy-start(pred[2304]{0:T(1024)(128)(4,1)} %get-tuple-element.401) | copy-start | bytes 6916
  133.1 14.0 %copy-start.10 = (pred[2304]{0:T(1024)(128)(4,1)S(1)}, pred[2304]{0:T(1024)(128)(4,1)}, u32[]{:S(2)}) copy-start(pred[2304]{0:T(1024)(128)(4,1)} %get-tuple-element.402) | copy-start | bytes 6916
  133.1 14.0 %copy-start.11 = (pred[2304]{0:T(1024)(128)(4,1)S(1)}, pred[2304]{0:T(1024)(128)(4,1)}, u32[]{:S(2)}) copy-start(pred[2304]{0:T(1024)(128)(4,1)} %get-tuple-element.403) | copy-start | bytes 6916
  133.1 14.0 %copy-start.12 = (pred[2304]{0:T(1024)(128)(4,1)S(1)}, pred[2304]{0:T(1024)(128)(4,1)}, u32[]{:S(2)}) copy-start(pred[2304]{0:T(1024)(128)(4,1)} %get-tuple-element.404) | copy-start | bytes 6916
where the time goes:
time: 156 us; the launch traced here: 155 us
  local copies, waits for them, and re-layouts  64.2 us (41%)
  starting transfers between devices  33 us (21%)
  other arithmetic  26.1 us (17%)
  waiting for transfers between devices  14 us (9%)
  matrix products  13.3 us (9%)
  loops' own time  3.73 us (2%)
    ppermute x4, starting transfers between devices, with_halo(): lax.ppermute(lax.slice_in_dim(block, 0, width, axis=dim), axis, backward)  16.8 us
    dot_general x12, matrix products, rotate_apply(): jnp.dot(matrix, data, precision=lax.Precision.HIGHEST, preferred_element_...  13.3 us
    reshape x10, local copies, waits for them, and re-layouts, rotate_apply(): return turned.reshape(middle, -1)  8.94 us
    all_to_all x1, waiting for transfers between devices, local(): lax.all_to_all(outgoing, 'slab', split_axis=3, concat_axis=0, tiled=True)  8.01 us
    slice x8, local copies, waits for them, and re-layouts, lateral_second(): jnp.roll(field, reach - width_x, -1)  7.53 us
    convert_element_type x1, other arithmetic, local(): return result.astype(jnp.bfloat16)  7.49 us
    all_to_all x1, starting transfers between devices, local(): lax.all_to_all(outgoing, 'slab', split_axis=3, concat_axis=0, tiled=True)  7.4 us
    slice x8, local copies, waits for them, and re-layouts, lateral_second(): jnp.roll(field, -reach * width_x, -1)  7.39 us
  transfers between devices with their start and end apart: 10, of which 4 were waited for; matrix products, arithmetic and copies ran while one was open for 62% of the time, Pallas kernels for 0%

commit v1 on v0

v1 whole, which is shorter than its diff:
```python
import functools
import math

import jax
import jax.numpy as jnp
import ml_dtypes
import numpy as np
from jax import lax
from jax.experimental import pallas as pl
from jax.experimental.pallas import tpu as pltpu
from jax.sharding import PartitionSpec as P

NX = 48
NY = 48
NZ = 64
NYX = NY * NX
LANES = 128
GROUP = 4
CHUNKS = 3

stencil_weights = (-205.0 / 72.0, 8.0 / 5.0, -1.0 / 5.0, 8.0 / 315.0, -1.0 / 560.0)
screening = 0.11
mixing = 0.25
MESH = pl.DeviceIdType.MESH


def squared_wave(length):
    grid = np.arange(length)
    folded = np.minimum(grid, length - grid).astype(np.float64)
    return (2.0 * math.pi * folded / length) ** 2


def screened_kernel():
    wave = (
        squared_wave(NX)[:, None, None]
        + squared_wave(NY)[None, :, None]
        + squared_wave(NZ)[None, None, :]
    )
    safe = np.where(wave > 0, wave, 1.0)
    inner = 4.0 * math.pi / safe * (1.0 - np.exp(-safe / (4.0 * screening * screening)))
    table = np.where(wave > 0, inner, math.pi / (screening * screening)) / (NX * NY * NZ)
    return np.concatenate([table, table], axis=2).astype(np.float32)


def split(matrix):
    high = matrix.astype(ml_dtypes.bfloat16)
    low = (matrix - high.astype(np.float64)).astype(ml_dtypes.bfloat16)
    return high, low


def hartley(length):
    grid = np.arange(length)
    angle = (grid[:, None] * grid[None, :] % length) * (2.0 * math.pi / length)
    return np.cos(angle) + np.sin(angle)


def left_table(length):
    high, low = split(hartley(length))
    return np.concatenate([high, low, high], axis=1)


def depth_table():
    high, low = split(np.kron(np.eye(2), hartley(NZ)))
    upper = np.concatenate([high, low], axis=1)
    lower = np.concatenate([high, np.zeros_like(low)], axis=1)
    return np.concatenate([upper, lower], axis=0)


def vertical_table():
    total = 3.0 * stencil_weights[0] * np.eye(NZ)
    for reach in range(1, 5):
        turned = np.roll(np.eye(NZ), reach, axis=0)
        total = total + stencil_weights[reach] * (turned + turned.T)
    high, low = split(-0.5 * total)
    return np.concatenate([high, low], axis=1)


def parts(data):
    high = data.astype(jnp.bfloat16)
    low = (data - high.astype(jnp.float32)).astype(jnp.bfloat16)
    return high, low


def from_left(table, data):
    high, low = parts(data)
    return jnp.dot(
        table, jnp.concatenate([high, high, low], axis=0), preferred_element_type=jnp.float32
    )


def from_right(data, table):
    high, low = parts(data)
    both = jnp.dot(
        jnp.concatenate([high, low], axis=1), table, preferred_element_type=jnp.float32
    )
    return both[:, :LANES] + both[:, LANES:]


def lateral(field):
    column = lax.broadcasted_iota(jnp.int32, field.shape, 1) % NX
    total = jnp.zeros_like(field)
    for reach in range(1, 5):
        along_y = pltpu.roll(field, reach * NX, 1) + pltpu.roll(field, NYX - reach * NX, 1)
        upper = jnp.where(
            column + reach < NX,
            pltpu.roll(field, NYX - reach, 1),
            pltpu.roll(field, NX - reach, 1),
        )
        lower = jnp.where(
            column >= reach,
            pltpu.roll(field, reach, 1),
            pltpu.roll(field, NYX + reach - NX, 1),
        )
        total = total + (-0.5 * stencil_weights[reach]) * (along_y + upper + lower)
    return total


def body(
    slabs, orbs, depth,
    orb_ref, pot_ref, flag_ref, side_ref, deep_ref, vert_ref, green_ref,
    out_ref,
    landed, wide, lap, vbuf, wbuf, field_a, field_b, ready,
    in_send, in_recv, fwd_send, fwd_recv, v_send, v_recv, w_send, w_recv,
    out_send, out_recv, here_sem,
):
    me = lax.axis_index("slab")
    orb = lax.axis_index("orb")
    number = me * orbs + orb
    after = lax.rem(number + 1, slabs * orbs)
    before = lax.rem(number + slabs * orbs - 1, slabs * orbs)
    right = (after // orbs, lax.rem(after, orbs))
    left = (before // orbs, lax.rem(before, orbs))

    def ahead(k):
        return lax.rem(me + k, slabs)

    def behind(k):
        return lax.rem(me + slabs - k, slabs)

    def remote(src, dst, send, recv, device):
        return pltpu.make_async_remote_copy(
            src_ref=src, dst_ref=dst, send_sem=send, recv_sem=recv,
            device_id=device, device_id_type=MESH,
        )

    barrier = pltpu.get_barrier_semaphore()
    for k in range(1, slabs):
        pl.semaphore_signal(barrier, inc=1, device_id=(ahead(k), orb), device_id_type=MESH)
    for device in (left, right):
        pl.semaphore_signal(barrier, inc=1, device_id=device, device_id_type=MESH)
    own_in = pltpu.make_async_copy(orb_ref.at[me], landed.at[1, me], here_sem.at[0])
    own_in.start()
    own_v = pltpu.make_async_copy(pot_ref, vbuf.at[me], here_sem.at[1])
    own_v.start()
    pl.semaphore_wait(barrier, slabs + 1)

    sends = []

    def start(copy):
        copy.start()
        sends.append(copy)
        return copy

    for k in range(1, slabs):
        start(remote(orb_ref.at[ahead(k)], landed.at[1, me], in_send.at[k], in_recv.at[k],
                     (ahead(k), orb)))

    def forward(k):
        source = behind(k)
        start(remote(landed.at[1, source], landed.at[0, source], fwd_send.at[0, k],
                     fwd_recv.at[0, k], right))
        start(remote(landed.at[1, source], landed.at[2, source], fwd_send.at[1, k],
                     fwd_recv.at[1, k], left))

    own_in.wait()
    forward(0)
    start(remote(flag_ref, wbuf.at[0], w_send.at[0], w_recv.at[0], right))
    start(remote(flag_ref, wbuf.at[1], w_send.at[1], w_recv.at[1], left))
    for k in range(1, slabs):
        source = behind(k)
        remote(orb_ref.at[me], landed.at[1, source], in_send.at[k], in_recv.at[k],
               (source, orb)).wait_recv()
        forward(k)
    own_v.wait()
    for k in range(1, slabs):
        start(remote(pot_ref, vbuf.at[me], v_send.at[k], v_recv.at[k], (ahead(k), orb)))

    for s in range(slabs):
        wide[1, s * depth : (s + 1) * depth, :] = landed[1, s].astype(jnp.float32)

    def lateral_turn(r, carry):
        rows = pl.ds(pl.multiple_of(r * 8, 8), 8)
        lap[rows, :] = lateral(wide[1, rows, :])
        return carry

    lax.fori_loop(0, NZ // 8, lateral_turn, 0)

    def vertical_turn(j, carry):
        lanes = pl.ds(pl.multiple_of(j * 256, 256), 256)
        values = wide[1, :, lanes].astype(jnp.bfloat16)
        lap[:, lanes] += jnp.dot(
            vert_ref[...], jnp.concatenate([values, values], axis=0),
            preferred_element_type=jnp.float32,
        )
        return carry

    lax.fori_loop(0, NYX // 256, vertical_turn, 0)

    for k in range(slabs):
        for side, sender in ((0, left), (1, right)):
            remote(landed.at[1, k], landed.at[2 * side, (sender[0] + slabs - k) % slabs],
                   fwd_send.at[side, k], fwd_recv.at[side, k], sender).wait_recv()
    for s in range(slabs):
        for side in (0, 2):
            wide[side, s * depth : (s + 1) * depth, :] = landed[side, s].astype(jnp.float32)

    def turn_in(j, carry):
        for t in range(2):
            lanes = pl.ds(pl.multiple_of((2 * j + t) * LANES, LANES), LANES)
            own = wide[1, :, lanes]
            stacked = jnp.concatenate([own * wide[2, :, lanes], own * wide[0, :, lanes]], axis=0)
            field_a[lanes, :] = stacked.T
        return carry

    lax.fori_loop(0, NYX // LANES // 2, turn_in, 0)

    def along_x(source, target):
        def turn(i, carry):
            base = i * (2 * GROUP)
            loaded = []
            for g in range(GROUP):
                halves = [
                    source[pl.ds(pl.multiple_of((base + 2 * g + t) * NX, NX), NX), :]
                    for t in range(2)
                ]
                loaded.append(jnp.concatenate(halves, axis=1))
            done = [from_left(side_ref[...], data) for data in loaded]
            for g in range(GROUP):
                for t in range(2):
                    rows = pl.ds(pl.multiple_of((base + 2 * g + t) * NX, NX), NX)
                    target[rows, :] = done[g][:, t * LANES : (t + 1) * LANES]
            return carry

        lax.fori_loop(0, NY // (2 * GROUP), turn, 0)

    def along_yz(source, target):
        def turn(i, carry):
            base = i * (2 * GROUP)
            data = []
            for g in range(GROUP):
                halves = [source[pl.ds(base + 2 * g + t, NY, stride=NX), :] for t in range(2)]
                data.append(jnp.concatenate(halves, axis=1))
            data = [from_left(side_ref[...], d) for d in data]
            data = [jnp.concatenate([d[:, :LANES], d[:, LANES:]], axis=0) for d in data]
            data = [from_right(d, deep_ref[...]) for d in data]
            greens = [
                jnp.concatenate([green_ref[base + 2 * g], green_ref[base + 2 * g + 1]], axis=0)
                for g in range(GROUP)
            ]
            data = [d * green for d, green in zip(data, greens)]
            data = [from_right(d, deep_ref[...]) for d in data]
            data = [jnp.concatenate([d[:NY], d[NY:]], axis=1) for d in data]
            data = [from_left(side_ref[...], d) for d in data]
            for g in range(GROUP):
                for t in range(2):
                    target[pl.ds(base + 2 * g + t, NY, stride=NX), :] = data[g][
                        :, t * LANES : (t + 1) * LANES
                    ]
            return carry

        lax.fori_loop(0, NX // (2 * GROUP), turn, 0)

    along_x(field_a, field_b)
    along_yz(field_b, field_a)
    along_x(field_a, field_b)

    for k in range(1, slabs):
        source = behind(k)
        remote(pot_ref, vbuf.at[source], v_send.at[k], v_recv.at[k], (source, orb)).wait_recv()
    remote(flag_ref, wbuf.at[0], w_send.at[0], w_recv.at[0], left).wait_recv()
    remote(flag_ref, wbuf.at[1], w_send.at[1], w_recv.at[1], right).wait_recv()
    weight_next = -mixing * (flag_ref[0, 0:1, :] + wbuf[1, 1, 0:1, :])
    weight_last = -mixing * (flag_ref[1, 0:1, :] + wbuf[0, 0, 0:1, :])

    span = NYX // CHUNKS

    def turn_out(j, carry):
        lanes = pl.ds(pl.multiple_of(j * LANES, LANES), LANES)
        pots = field_b[lanes, :].T
        terms = (
            lap[:, lanes]
            + weight_next * (pots[:NZ] * wide[2, :, lanes])
            + weight_last * (pots[NZ:] * wide[0, :, lanes])
        )
        own = wide[1, :, lanes]
        for s in range(slabs):
            rows = slice(s * depth, (s + 1) * depth)
            ready[s, :, lanes] = (terms[rows] + vbuf[s, :, lanes] * own[rows]).astype(jnp.bfloat16)
        return carry

    tiles = span // LANES
    for c in range(CHUNKS):
        lax.fori_loop(c * tiles, (c + 1) * tiles, turn_out, 0)
        lanes = pl.ds(c * span, span)
        for k in range(1, slabs):
            peer = ahead(k)
            start(remote(ready.at[peer, :, lanes], out_ref.at[me, :, lanes], out_send.at[c, k],
                         out_recv.at[c, k], (peer, orb)))
    own_out = pltpu.make_async_copy(ready.at[me], out_ref.at[me], here_sem.at[0])
    own_out.start()
    for c in range(CHUNKS):
        lanes = pl.ds(c * span, span)
        for k in range(1, slabs):
            source = behind(k)
            remote(ready.at[me, :, lanes], out_ref.at[source, :, lanes], out_send.at[c, k],
                   out_recv.at[c, k], (source, orb)).wait_recv()
    for copy in sends:
        copy.wait_send()
    own_out.wait()


def local(orbitals, potential, partners, pair_valid):
    slabs, depth = orbitals.shape[0], orbitals.shape[3]
    orbs = lax.axis_size("orb")
    flags = jnp.broadcast_to(
        pair_valid.reshape(2, 1, 1).astype(jnp.float32), (2, 8, LANES)
    )
    dma = pltpu.SemaphoreType.DMA
    any_space = pl.BlockSpec(memory_space=pl.ANY)
    vmem = pl.BlockSpec(memory_space=pltpu.VMEM)
    result = pl.pallas_call(
        functools.partial(body, slabs, orbs, depth),
        out_shape=jax.ShapeDtypeStruct((slabs, depth, NYX), jnp.bfloat16),
        in_specs=[any_space, any_space, vmem, vmem, vmem, vmem, vmem],
        out_specs=any_space,
        scratch_shapes=[
            pltpu.VMEM((3, slabs, depth, NYX), jnp.bfloat16),
            pltpu.VMEM((3, NZ, NYX), jnp.float32),
            pltpu.VMEM((NZ, NYX), jnp.float32),
            pltpu.VMEM((slabs, depth, NYX), jnp.float32),
            pltpu.VMEM((2, 2, 8, LANES), jnp.float32),
            pltpu.VMEM((NYX, LANES), jnp.float32),
            pltpu.VMEM((NYX, LANES), jnp.float32),
            pltpu.VMEM((slabs, depth, NYX), jnp.bfloat16),
            dma((slabs,)), dma((slabs,)),
            dma((2, slabs)), dma((2, slabs)),
            dma((slabs,)), dma((slabs,)),
            dma((2,)), dma((2,)),
            dma((CHUNKS, slabs)), dma((CHUNKS, slabs)),
            dma((2,)),
        ],
        compiler_params=pltpu.CompilerParams(
            collective_id=0, has_side_effects=True, vmem_limit_bytes=40 * 1024 * 1024
        ),
        cost_estimate=pl.CostEstimate(
            flops=2 * 1024 * 1024 * 1024, bytes_accessed=8 * 1024 * 1024, transcendentals=0
        ),
    )(
        orbitals.reshape(slabs, depth, NYX), potential, flags,
        jnp.asarray(left_table(NX)), jnp.asarray(depth_table()), jnp.asarray(vertical_table()),
        jnp.asarray(screened_kernel()),
    )
    return result.reshape(orbitals.shape)


def solution(mesh):
    in_specs = (
        P(None, "orb", None, "slab", None),
        P("slab", None),
        P("slab", "orb", None, None),
        P("slab", "orb", None, None),
    )
    out_specs = P(None, "orb", None, "slab", None)
    return jax.shard_map(local, mesh=mesh, in_specs=in_specs, out_specs=out_specs, check_vma=False)
```

time: 156 us -> 49.9 us (0.32)
  local copies, waits for them, and re-layouts: 64.2 us -> 6.26 us
  Pallas kernels: 0 us -> 42.6 us
  starting transfers between devices: 33 us -> 0 us
  other arithmetic: 26.1 us -> 0.66 us
  waiting for transfers between devices: 14 us -> 0 us
  matrix products: 13.3 us -> 0 us
  loops' own time: 3.73 us -> 0 us
    pallas_call x0 -> x1, Pallas kernels: none -> 42.6 us  [local(): pl.pallas_call(functools.partial(body, slabs, orbs, depth), out_shape=jax...]
    slice x26 -> x0, local copies, waits for them, and re-layouts: 25.3 us -> none  [the longest x8 7.53 us: lateral_second(): jnp.roll(field, reach - width_x, -1)]
    ppermute x8 -> x0, starting transfers between devices: 19.9 us -> none  [the longest x4 16.8 us: with_halo(): lax.ppermute(lax.slice_in_dim(block, 0, width, axis=dim), axis, backward)]
    reshape x20 -> x0, local copies, waits for them, and re-layouts: 16 us -> none  [the longest x10 8.94 us: rotate_apply(): return turned.reshape(middle, -1)]
    dot_general x12 -> x0, matrix products: 13.3 us -> none  [rotate_apply(): jnp.dot(matrix, data, precision=lax.Precision.HIGHEST, preferred_element_...]
    all_to_all x2 -> x0, starting transfers between devices: 13.1 us -> none  [the longest x1 7.4 us: local(): lax.all_to_all(outgoing, 'slab', split_axis=3, concat_axis=0, tiled=True)]
    scatter-add x4 -> x0, other arithmetic: 10.8 us -> none  [the longest x2 5.48 us: pair_turn(): accum = accum.at[partner_row].add(field * first)]
    all_to_all x2 -> x0, waiting for transfers between devices: 8.02 us -> none  [the longest x1 8.01 us: local(): lax.all_to_all(outgoing, 'slab', split_axis=3, concat_axis=0, tiled=True)]
  transfers between devices with their start and end apart: 10 -> 0, of which waited for: 4 -> 0; matrix products, arithmetic and copies ran while one was open for 62% -> 0% of each run, Pallas kernels for 0% -> 0%
where the time goes in v1:
time: 49.9 us; the launch traced here: 49.5 us
  Pallas kernels  42.6 us (85%)
  local copies, waits for them, and re-layouts  6.26 us (13%)
  other arithmetic  0.66 us (1%)
    pallas_call x1, Pallas kernels, local(): pl.pallas_call(functools.partial(body, slabs, orbs, depth), out_shape=jax...  42.6 us
    unnamed x13, local copies, waits for them, and re-layouts  6.19 us

profile of v1, /device:TPU:5, one launch (start us, length us, event | category | flops | bytes accessed | tf_op | source)
XLA Modules:
  0.0 49.5 jit_solution(4644624710111927310)
XLA Ops:
  0.0 0.7 %convert_bitcast_fusion = f32[2]{0:T(128)S(1)} fusion(s32[1,1,1,2]{3,2,1,0:T(1,128)} %param.10), kind=kLoop, calls=%fused_computation | loop fusion | flops 2 | bytes 16 | tf_op jit(solution)/shard_map/convert_element_type | solution.py:326
  0.7 0.1 broadcast_in_dim.2.flag_ref
  0.7 0.0 copy-start
  0.7 1.0 %copy-done = bf16[8,1,1,8,2304]{4,3,2,1,0:T(8,128)(2,1)S(1)} copy-done((bf16[8,1,1,8,2304]{4,3,2,1,0:T(8,128)(2,1)S(1)}, bf16[8,1,1,8,2304]{4,3,2,1,0:T(8,128)(2,1)}, u32[]{:S(2)}) %copy-start) | copy-done | bytes 294936
  1.7 0.0 copy-start.1
  1.7 0.9 %copy-done.1 = f32[8,2304]{1,0:T(8,128)S(1)} copy-done((f32[8,2304]{1,0:T(8,128)S(1)}, f32[8,2304]{1,0:T(8,128)}, u32[]{:S(2)}) %copy-start.1) | copy-done | bytes 73752
  2.6 0.0 copy-start.2
  2.6 1.3 %copy-done.2 = f32[48,48,128]{2,1,0:T(8,128)S(1)} copy-done((f32[48,48,128]{2,1,0:T(8,128)S(1)}, f32[48,48,128]{2,1,0:T(8,128)}, u32[]{:S(2)}) %copy-start.2) | copy-done | bytes 1179672
  3.9 0.0 copy-start.3
  3.9 0.9 %copy-done.3 = bf16[256,256]{1,0:T(8,128)(2,1)S(1)} copy-done((bf16[256,256]{1,0:T(8,128)(2,1)S(1)}, bf16[256,256]{1,0:T(8,128)(2,1)}, u32[]{:S(2)}) %copy-start.3) | copy-done | bytes 131096
  4.8 0.0 copy-start.4
  4.8 0.7 %copy-done.4 = bf16[48,144]{1,0:T(8,128)(2,1)S(1)} copy-done((bf16[48,144]{1,0:T(8,128)(2,1)S(1)}, bf16[48,144]{1,0:T(8,128)(2,1)}, u32[]{:S(2)}) %copy-start.4) | copy-done | bytes 13848
  5.5 0.0 copy-start.5
  5.5 0.7 %copy-done.5 = bf16[64,128]{1,0:T(8,128)(2,1)S(1)} copy-done((bf16[64,128]{1,0:T(8,128)(2,1)S(1)}, bf16[64,128]{1,0:T(8,128)(2,1)}, u32[]{:S(2)}) %copy-start.5) | copy-done | bytes 16408
  6.2 42.6 %shard_map.73 = bf16[8,8,2304]{2,1,0:T(8,128)(2,1)S(1)} custom-call(bf16[8,8,2304]{2,1,0:T(8,128)(2,1)S(1)} %bitcast.7, f32[8,2304]{1,0:T(8,128)S(1)} %copy-done.1, f32[2,8,128]{2,1,0:T(8,128)S(1)} %broadcast_in_dim.2.flag_ref, bf16[48,144]{1,0:T(8,128)(2,1)S(1)} %copy-done.4, bf16[256,256]{1,0:T(8,128)(2,1)S(1)} %copy-done.3, ...), custom_call_target="tpu_custom_call" | custom-call | flops 2147483648 | bytes 8388608 | tf_op jit(solution)/shard_map/pallas_call | solution.py:331
  48.8 0.7 %copy.10 = bf16[8,1,1,8,2304]{4,3,2,1,0:T(8,128)(2,1)} copy(bf16[8,1,1,8,2304]{4,3,2,1,0:T(8,128)(2,1)S(1)} %bitcast.6) | data formatting | bytes 589824
Async XLA Ops:
  0.7 1.0 %copy-start = (bf16[8,1,1,8,2304]{4,3,2,1,0:T(8,128)(2,1)S(1)}, bf16[8,1,1,8,2304]{4,3,2,1,0:T(8,128)(2,1)}, u32[]{:S(2)}) copy-start(bf16[8,1,1,8,2304]{4,3,2,1,0:T(8,128)(2,1)} %param.8) | copy-start | bytes 884740
  1.7 0.9 %copy-start.1 = (f32[8,2304]{1,0:T(8,128)S(1)}, f32[8,2304]{1,0:T(8,128)}, u32[]{:S(2)}) copy-start(f32[8,2304]{1,0:T(8,128)} %pot_ref.1) | copy-start | bytes 221188
  2.6 1.3 %copy-start.2 = (f32[48,48,128]{2,1,0:T(8,128)S(1)}, f32[48,48,128]{2,1,0:T(8,128)}, u32[]{:S(2)}) copy-start(f32[48,48,128]{2,1,0:T(8,128)} %constant.11.clone.green_ref) | copy-start | bytes 3538948
  3.9 0.9 %copy-start.3 = (bf16[256,256]{1,0:T(8,128)(2,1)S(1)}, bf16[256,256]{1,0:T(8,128)(2,1)}, u32[]{:S(2)}) copy-start(bf16[256,256]{1,0:T(8,128)(2,1)} %constant.9.clone.deep_ref) | copy-start | bytes 393220
  4.8 0.7 %copy-start.4 = (bf16[48,144]{1,0:T(8,128)(2,1)S(1)}, bf16[48,144]{1,0:T(8,128)(2,1)}, u32[]{:S(2)}) copy-start(bf16[48,144]{1,0:T(8,128)(2,1)} %constant.8.clone.side_ref) | copy-start | bytes 41476
  5.5 0.7 %copy-start.5 = (bf16[64,128]{1,0:T(8,128)(2,1)S(1)}, bf16[64,128]{1,0:T(8,128)(2,1)}, u32[]{:S(2)}) copy-start(bf16[64,128]{1,0:T(8,128)(2,1)} %constant.10.clone.vert_ref) | copy-start | bytes 49156

commit v2 on v1

--- a/solution.py
+++ b/solution.py
@@ -117,9 +117,10 @@
 
 def body(
     slabs, orbs, depth,
-    orb_ref, pot_ref, flag_ref, side_ref, deep_ref, vert_ref, green_ref,
+    orb_ref, pot_ref, valid_ref, side_hbm, deep_hbm, vert_hbm, green_hbm,
     out_ref,
     landed, wide, lap, vbuf, wbuf, field_a, field_b, ready,
+    flag_ref, side_ref, deep_ref, vert_ref, green_ref,
     in_send, in_recv, fwd_send, fwd_recv, v_send, v_recv, w_send, w_recv,
     out_send, out_recv, here_sem,
 ):
@@ -148,10 +149,25 @@
         pl.semaphore_signal(barrier, inc=1, device_id=(ahead(k), orb), device_id_type=MESH)
     for device in (left, right):
         pl.semaphore_signal(barrier, inc=1, device_id=device, device_id_type=MESH)
+    half = NYX // 2
+    mine = pl.ds(pl.multiple_of(lax.rem(orb, 2) * half, LANES), half)
+    other = pl.ds(pl.multiple_of((1 - lax.rem(orb, 2)) * half, LANES), half)
+    sibling = (me, orb + 1 - 2 * lax.rem(orb, 2))
     own_in = pltpu.make_async_copy(orb_ref.at[me], landed.at[1, me], here_sem.at[0])
     own_in.start()
-    own_v = pltpu.make_async_copy(pot_ref, vbuf.at[me], here_sem.at[1])
+    own_v = pltpu.make_async_copy(pot_ref.at[:, mine], vbuf.at[me, :, mine], here_sem.at[1])
     own_v.start()
+    tables = [
+        pltpu.make_async_copy(source, target, here_sem.at[2 + t])
+        for t, (source, target) in enumerate(
+            ((vert_hbm, vert_ref), (side_hbm, side_ref), (deep_hbm, deep_ref), (green_hbm, green_ref))
+        )
+    ]
+    for table in tables:
+        table.start()
+    for slot in range(2):
+        flag = jnp.full((8, LANES), valid_ref[0, 0, 0, slot], jnp.int32)
+        flag_ref[slot] = flag.astype(jnp.float32)
     pl.semaphore_wait(barrier, slabs + 1)
 
     sends = []
@@ -161,58 +177,58 @@
         sends.append(copy)
         return copy
 
-    for k in range(1, slabs):
-        start(remote(orb_ref.at[ahead(k)], landed.at[1, me], in_send.at[k], in_recv.at[k],
-                     (ahead(k), orb)))
-
-    def forward(k):
-        source = behind(k)
-        start(remote(landed.at[1, source], landed.at[0, source], fwd_send.at[0, k],
-                     fwd_recv.at[0, k], right))
-        start(remote(landed.at[1, source], landed.at[2, source], fwd_send.at[1, k],
-                     fwd_recv.at[1, k], left))
-
-    own_in.wait()
-    forward(0)
+    span = NYX // CHUNKS
+    tiles = span // LANES
+    rows_each = span // NX
+
+    def part(c):
+        return pl.ds(c * span, span)
+
+    for c in range(CHUNKS):
+        for k in range(1, slabs):
+            start(remote(orb_ref.at[ahead(k), :, part(c)], landed.at[1, me, :, part(c)],
+                         in_send.at[c, k], in_recv.at[c, k], (ahead(k), orb)))
     start(remote(flag_ref, wbuf.at[0], w_send.at[0], w_recv.at[0], right))
     start(remote(flag_ref, wbuf.at[1], w_send.at[1], w_recv.at[1], left))
-    for k in range(1, slabs):
-        source = behind(k)
-        remote(orb_ref.at[me], landed.at[1, source], in_send.at[k], in_recv.at[k],
-               (source, orb)).wait_recv()
-        forward(k)
-    own_v.wait()
-    for k in range(1, slabs):
-        start(remote(pot_ref, vbuf.at[me], v_send.at[k], v_recv.at[k], (ahead(k), orb)))
-
-    for s in range(slabs):
-        wide[1, s * depth : (s + 1) * depth, :] = landed[1, s].astype(jnp.float32)
-
-    def lateral_turn(r, carry):
-        rows = pl.ds(pl.multiple_of(r * 8, 8), 8)
-        lap[rows, :] = lateral(wide[1, rows, :])
-        return carry
-
-    lax.fori_loop(0, NZ // 8, lateral_turn, 0)
+    own_in.wait()
+
+    def unpack(side, c):
+        for s in range(slabs):
+            wide[side, s * depth : (s + 1) * depth, c * span : (c + 1) * span] = landed[
+                side, s, :, c * span : (c + 1) * span
+            ].astype(jnp.float32)
 
     def vertical_turn(j, carry):
         lanes = pl.ds(pl.multiple_of(j * 256, 256), 256)
         values = wide[1, :, lanes].astype(jnp.bfloat16)
-        lap[:, lanes] += jnp.dot(
+        lap[:, lanes] = jnp.dot(
             vert_ref[...], jnp.concatenate([values, values], axis=0),
             preferred_element_type=jnp.float32,
         )
         return carry
 
-    lax.fori_loop(0, NYX // 256, vertical_turn, 0)
-
-    for k in range(slabs):
-        for side, sender in ((0, left), (1, right)):
-            remote(landed.at[1, k], landed.at[2 * side, (sender[0] + slabs - k) % slabs],
-                   fwd_send.at[side, k], fwd_recv.at[side, k], sender).wait_recv()
-    for s in range(slabs):
-        for side in (0, 2):
-            wide[side, s * depth : (s + 1) * depth, :] = landed[side, s].astype(jnp.float32)
+    tables[0].wait()
+    for c in range(CHUNKS):
+        for k in range(1, slabs):
+            source = behind(k)
+            remote(orb_ref.at[me, :, part(c)], landed.at[1, source, :, part(c)],
+                   in_send.at[c, k], in_recv.at[c, k], (source, orb)).wait_recv()
+        start(remote(landed.at[1, :, :, part(c)], landed.at[0, :, :, part(c)],
+                     fwd_send.at[0, c], fwd_recv.at[0, c], right))
+        start(remote(landed.at[1, :, :, part(c)], landed.at[2, :, :, part(c)],
+                     fwd_send.at[1, c], fwd_recv.at[1, c], left))
+        if c == CHUNKS - 1:
+            own_v.wait()
+            for k in range(1, slabs):
+                start(remote(pot_ref.at[:, mine], vbuf.at[me, :, mine], v_send.at[k],
+                             v_recv.at[k], (ahead(k), orb)))
+        unpack(1, c)
+        lax.fori_loop(c * span // 256, (c + 1) * span // 256, vertical_turn, 0)
+
+    def lateral_turn(r, carry):
+        rows = pl.ds(pl.multiple_of(r * 8, 8), 8)
+        lap[rows, :] += lateral(wide[1, rows, :])
+        return carry
 
     def turn_in(j, carry):
         for t in range(2):
@@ -222,9 +238,7 @@
             field_a[lanes, :] = stacked.T
         return carry
 
-    lax.fori_loop(0, NYX // LANES // 2, turn_in, 0)
-
-    def along_x(source, target):
+    def along_x(source, target, c):
         def turn(i, carry):
             base = i * (2 * GROUP)
             loaded = []
@@ -241,7 +255,19 @@
                     target[rows, :] = done[g][:, t * LANES : (t + 1) * LANES]
             return carry
 
-        lax.fori_loop(0, NY // (2 * GROUP), turn, 0)
+        each = rows_each // (2 * GROUP)
+        lax.fori_loop(c * each, (c + 1) * each, turn, 0)
+
+    tables[1].wait()
+    for c in range(CHUNKS):
+        if c == CHUNKS - 1:
+            lax.fori_loop(0, NZ // 8, lateral_turn, 0)
+        for side, sender in ((0, left), (1, right)):
+            remote(landed.at[1, :, :, part(c)], landed.at[2 * side, :, :, part(c)],
+                   fwd_send.at[side, c], fwd_recv.at[side, c], sender).wait_recv()
+            unpack(2 * side, c)
+        lax.fori_loop(c * tiles // 2, (c + 1) * tiles // 2, turn_in, 0)
+        along_x(field_a, field_b, c)
 
     def along_yz(source, target):
         def turn(i, carry):
@@ -270,19 +296,19 @@
 
         lax.fori_loop(0, NX // (2 * GROUP), turn, 0)
 
-    along_x(field_a, field_b)
+    tables[2].wait()
+    tables[3].wait()
     along_yz(field_b, field_a)
-    along_x(field_a, field_b)
 
     for k in range(1, slabs):
         source = behind(k)
-        remote(pot_ref, vbuf.at[source], v_send.at[k], v_recv.at[k], (source, orb)).wait_recv()
+        remote(pot_ref.at[:, mine], vbuf.at[source, :, mine], v_send.at[k], v_recv.at[k],
+               (source, orb)).wait_recv()
+    start(remote(vbuf.at[:, :, mine], vbuf.at[:, :, mine], v_send.at[0], v_recv.at[0], sibling))
     remote(flag_ref, wbuf.at[0], w_send.at[0], w_recv.at[0], left).wait_recv()
     remote(flag_ref, wbuf.at[1], w_send.at[1], w_recv.at[1], right).wait_recv()
     weight_next = -mixing * (flag_ref[0, 0:1, :] + wbuf[1, 1, 0:1, :])
     weight_last = -mixing * (flag_ref[1, 0:1, :] + wbuf[0, 0, 0:1, :])
-
-    span = NYX // CHUNKS
 
     def turn_out(j, carry):
         lanes = pl.ds(pl.multiple_of(j * LANES, LANES), LANES)
@@ -298,8 +324,11 @@
             ready[s, :, lanes] = (terms[rows] + vbuf[s, :, lanes] * own[rows]).astype(jnp.bfloat16)
         return carry
 
-    tiles = span // LANES
     for c in range(CHUNKS):
+        along_x(field_a, field_b, c)
+        if c == 0:
+            remote(vbuf.at[:, :, mine], vbuf.at[:, :, other], v_send.at[0], v_recv.at[0],
+                   sibling).wait_recv()
         lax.fori_loop(c * tiles, (c + 1) * tiles, turn_out, 0)
         lanes = pl.ds(c * span, span)
         for k in range(1, slabs):
@@ -322,16 +351,12 @@
 def local(orbitals, potential, partners, pair_valid):
     slabs, depth = orbitals.shape[0], orbitals.shape[3]
     orbs = lax.axis_size("orb")
-    flags = jnp.broadcast_to(
-        pair_valid.reshape(2, 1, 1).astype(jnp.float32), (2, 8, LANES)
-    )
     dma = pltpu.SemaphoreType.DMA
     any_space = pl.BlockSpec(memory_space=pl.ANY)
-    vmem = pl.BlockSpec(memory_space=pltpu.VMEM)
     result = pl.pallas_call(
         functools.partial(body, slabs, orbs, depth),
         out_shape=jax.ShapeDtypeStruct((slabs, depth, NYX), jnp.bfloat16),
-        in_specs=[any_space, any_space, vmem, vmem, vmem, vmem, vmem],
+        in_specs=[any_space, any_space, pl.BlockSpec(memory_space=pltpu.SMEM)] + [any_space] * 4,
         out_specs=any_space,
         scratch_shapes=[
             pltpu.VMEM((3, slabs, depth, NYX), jnp.bfloat16),
@@ -342,21 +367,26 @@
             pltpu.VMEM((NYX, LANES), jnp.float32),
             pltpu.VMEM((NYX, LANES), jnp.float32),
             pltpu.VMEM((slabs, depth, NYX), jnp.bfloat16),
-            dma((slabs,)), dma((slabs,)),
-            dma((2, slabs)), dma((2, slabs)),
+            pltpu.VMEM((2, 8, LANES), jnp.float32),
+            pltpu.VMEM((NX, 3 * NX), jnp.bfloat16),
+            pltpu.VMEM((4 * NZ, 4 * NZ), jnp.bfloat16),
+            pltpu.VMEM((NZ, 2 * NZ), jnp.bfloat16),
+            pltpu.VMEM((NX, NY, LANES), jnp.float32),
+            dma((CHUNKS, slabs)), dma((CHUNKS, slabs)),
+            dma((2, CHUNKS)), dma((2, CHUNKS)),
             dma((slabs,)), dma((slabs,)),
             dma((2,)), dma((2,)),
             dma((CHUNKS, slabs)), dma((CHUNKS, slabs)),
-            dma((2,)),
+            dma((6,)),
         ],
         compiler_params=pltpu.CompilerParams(
-            collective_id=0, has_side_effects=True, vmem_limit_bytes=40 * 1024 * 1024
+            collective_id=0, has_side_effects=True, vmem_limit_bytes=60 * 1024 * 1024
         ),
         cost_estimate=pl.CostEstimate(
             flops=2 * 1024 * 1024 * 1024, bytes_accessed=8 * 1024 * 1024, transcendentals=0
         ),
     )(
-        orbitals.reshape(slabs, depth, NYX), potential, flags,
+        orbitals.reshape(slabs, depth, NYX), potential, pair_valid,
         jnp.asarray(left_table(NX)), jnp.asarray(depth_table()), jnp.asarray(vertical_table()),
         jnp.asarray(screened_kernel()),
     )

time: 49.9 us -> 42 us (0.84)
  the two profiles are of different devices: /device:TPU:5 before, /device:TPU:0 now
where the time goes in v2:
time: 42 us; the launch traced here: 41.9 us
  Pallas kernels  40.1 us (95%)
  local copies, waits for them, and re-layouts  1.69 us (4%)
    pallas_call x1, Pallas kernels, local(): pl.pallas_call(functools.partial(body, slabs, orbs, depth), out_shape=jax...  40.1 us
    unnamed x1, local copies, waits for them, and re-layouts  1.69 us

profile of v2, /device:TPU:0, one launch (start us, length us, event | category | flops | bytes accessed | tf_op | source)
XLA Modules:
  0.0 41.9 jit_solution(6271899302302743198)
XLA Ops:
  0.0 40.1 %shard_map.73 = bf16[8,8,2304]{2,1,0:T(8,128)(2,1)} custom-call(bf16[8,8,2304]{2,1,0:T(8,128)(2,1)} %bitcast.5, f32[8,2304]{1,0:T(8,128)} %pot_ref.1, s32[1,1,1,2]{3,2,1,0:T(1,128)} %valid_ref.1, bf16[48,144]{1,0:T(8,128)(2,1)} %constant.8.clone.side_hbm, bf16[256,256]{1,0:T(8,128)(2,1)} %constant.9.clone.deep_hbm, bf16[64,128]{1,0:T(8,128)(2,1)} %constant.10.clone.vert_hbm, ...), custom_call_target="tpu_custom_call" | custom-call | flops 2147483648 | bytes 8388608 | tf_op jit(solution)/shard_map/pallas_call | solution.py:356
  40.2 1.7 %copy.10 = bf16[8,1,1,8,2304]{4,3,2,1,0:T(8,128)(2,1)} copy(bf16[8,1,1,8,2304]{4,3,2,1,0:T(8,128)(2,1)} %bitcast.4) | data formatting | bytes 589824
